TPU v7x, 512 devices: a whole 4x4x16 slice. The times are simulated.
512 devices in a mesh: tm: 32 (over x, y, core), tile: 16 (over z).
Axes of the slice: x: 4, y: 4, z: 16, core: 2. Of those that a mesh axis runs over, the one named last changes fastest.
Arguments:
- seg_gain: bfloat16 [32, 1024, 1024], P('tm', 'tile'), may hold values from -0.1875 to 0.1875
- seg_offset: float32 [32, 1024], P('tm', 'tile'), may hold values from -6 to 6
- seg_noise: bfloat16 [32, 1024, 1024], P('tm', 'tile'), as said below
- end_mean: bfloat16 [8, 1024], P(None, 'tile'), may hold values from -6 to 6
- end_cov: bfloat16 [8, 1024, 1024], P(None, 'tile'), as said below
- step_gain: bfloat16 [256, 1024, 1024], P('tm', 'tile'), may hold values from -0.1875 to 0.1875
- step_offset: float32 [256, 1024], P('tm', 'tile'), may hold values from -6 to 6
- step_var: float32 [256, 1024], P('tm', 'tile'), may hold values from 0.1 to 1.5
- obs_tiles: int32 [256, 4], P('tm'), may hold values from 0 to 7
- obs_count: int32 [256], P('tm'), may hold values from 1 to 4, as said below
- obs_value: float32 [256, 4, 128], P('tm'), may hold values from -10 to 10
- obs_noise: float32 [1024], replicated, may hold values from 0.2 to 2
Outputs:
- start_cov: bfloat16 [32, 1024, 1024], P('tm', 'tile')
- start_mean: bfloat16 [32, 1024], P('tm', 'tile')
- step_mean: float32 [256, 1024], P('tm', 'tile')
- step_spread: float32 [256, 1024], P('tm', 'tile')
- innovation: float32 [256, 4, 128], P('tm')
Inputs may be any that keep to these rules, and one draw needn't show every extreme that they name: `end_cov`: each matrix is symmetric and positive definite. `seg_noise`: each matrix is symmetric and positive definite. `obs_count`: some step has 4 live slots and some has 1.
All inputs are finite; a program needn't handle non-finite values.
Results may differ from a plain program's by a relative error of at most 0.015.
Values may be sent and summed in bfloat16 or wider, within the bound.
A program may use at most 64 MiB of HBM per device.

v0:
```python
import jax
import jax.numpy as jnp
from jax import lax
from jax.sharding import PartitionSpec as P

TILE_STATES = 128
SLOTS = 4
GROUP_SEGS = 4


def shifted(block, axis, distance):
    devices = range(lax.axis_size(axis))
    route = [(i - distance, i) for i in devices if i - distance in devices]
    return lax.ppermute(block, axis, route)


def shards(
    seg_gain,
    seg_offset,
    seg_noise,
    end_mean,
    end_cov,
    step_gain,
    step_offset,
    step_var,
    obs_tiles,
    obs_count,
    obs_value,
    obs_noise,
):
    position = lax.axis_index("tm")
    slot_place = position % GROUP_SEGS
    group_index = position // GROUP_SEGS
    gain_rows = seg_gain[0]
    offset_rows = seg_offset[0]
    noise_rows = seg_noise[0].astype(jnp.float32)
    row_count = gain_rows.shape[0]
    state_count = gain_rows.shape[1]
    cur_mean = lax.dynamic_index_in_dim(end_mean, group_index, 0, keepdims=False)
    cur_cov = lax.dynamic_index_in_dim(end_cov, group_index, 0, keepdims=False)
    kept_mean = jnp.zeros((state_count,), jnp.bfloat16)
    kept_cov = jnp.zeros((state_count, state_count), jnp.bfloat16)
    out_mean = jnp.zeros((row_count,), jnp.bfloat16)
    out_cov = jnp.zeros((row_count, state_count), jnp.bfloat16)
    for depth_step in range(GROUP_SEGS):
        whole_mean, whole_cov = (
            lax.all_gather(cur_mean, "tile", axis=0, tiled=True),
            lax.all_gather(cur_cov, "tile", axis=0, tiled=True),
        )
        is_mine = slot_place == GROUP_SEGS - 1 - depth_step
        kept_mean = jnp.where(is_mine, whole_mean, kept_mean)
        kept_cov = jnp.where(is_mine, whole_cov, kept_cov)
        product = jnp.dot(gain_rows, whole_cov, preferred_element_type=jnp.float32).astype(
            jnp.bfloat16
        )
        col_block = jnp.einsum(
            "pd,rd->pr",
            lax.all_gather(product, "tile", axis=0, tiled=True),
            gain_rows,
            preferred_element_type=jnp.float32,
        )
        spread_rows = lax.all_to_all(col_block, "tile", split_axis=0, concat_axis=1, tiled=True)
        new_cov = (spread_rows + noise_rows).astype(jnp.bfloat16)
        new_mean = (
            jnp.dot(gain_rows, whole_mean, preferred_element_type=jnp.float32) + offset_rows
        ).astype(jnp.bfloat16)
        out_mean = jnp.where(is_mine, new_mean, out_mean)
        out_cov = jnp.where(is_mine, new_cov, out_cov)
        if depth_step < GROUP_SEGS - 1:
            got_mean, got_cov = shifted((new_mean, new_cov), "tm", -1)
            takes_next = slot_place == GROUP_SEGS - 2 - depth_step
            cur_mean = jnp.where(takes_next, got_mean, cur_mean)
            cur_cov = jnp.where(takes_next, got_cov, cur_cov)
    partial_value = jnp.einsum(
        "krd,de->kre", step_gain, kept_cov, preferred_element_type=jnp.float32
    )
    local_spread = jnp.sum(partial_value * step_gain, axis=2) + step_var
    local_mean = (
        jnp.einsum("krd,d->kr", step_gain, kept_mean, preferred_element_type=jnp.float32)
        + step_offset
    )
    full_mean, full_spread = (
        lax.all_gather(local_mean, "tile", axis=1, tiled=True),
        lax.all_gather(local_spread, "tile", axis=1, tiled=True),
    )
    step_count = full_mean.shape[0]
    tile_total = state_count // TILE_STATES
    tile_mean = full_mean.reshape(step_count, tile_total, TILE_STATES)
    tile_spread = full_spread.reshape(step_count, tile_total, TILE_STATES) + obs_noise.reshape(
        1, tile_total, TILE_STATES
    )
    onehot = (
        obs_tiles[:, :, None] == jnp.arange(tile_total, dtype=jnp.int32)[None, None, :]
    ).astype(jnp.float32)
    picked_mean = jnp.einsum("ksn,kno->kso", onehot, tile_mean, precision=lax.Precision.HIGHEST)
    picked_spread = jnp.einsum("ksn,kno->kso", onehot, tile_spread, precision=lax.Precision.HIGHEST)
    live_slots = jnp.arange(SLOTS, dtype=jnp.int32)[None, :] < obs_count[:, None]
    innovation = jnp.where(
        live_slots[:, :, None], (obs_value - picked_mean) / picked_spread, jnp.float32(0.0)
    )
    return (out_cov[None], out_mean[None], local_mean, local_spread, innovation)


def solution(mesh):
    in_specs = (
        P("tm", "tile", None),
        P("tm", "tile"),
        P("tm", "tile", None),
        P(None, "tile"),
        P(None, "tile", None),
        P("tm", "tile", None),
        P("tm", "tile"),
        P("tm", "tile"),
        P("tm", None),
        P("tm"),
        P("tm", None, None),
        P(),
    )
    out_specs = (
        P("tm", "tile", None),
        P("tm", "tile"),
        P("tm", "tile"),
        P("tm", "tile"),
        P("tm", None, None),
    )
    return jax.shard_map(shards, mesh=mesh, in_specs=in_specs, out_specs=out_specs, check_vma=False)
```

profile of v0, /device:TPU:4, one launch (start us, length us, event | category | flops | bytes accessed | tf_op | source)
XLA Modules:
  0.0 827.4 jit_solution(18395162919575817385)
XLA Ops:
  8.9 79.3 %all-gather.27.cloned.1.call-done = bf16[1,1024,1024]{2,1,0:T(8,128)(2,1)} async-done(((bf16[1,64,1024]{2,1,0:T(8,128)(2,1)}), bf16[1,1024,1024]{2,1,0:T(8,128)(2,1)}) %all-gather.27.cloned.1.call-update) | async-done | bytes 2097168 | tf_op jit(solution)/shard_map/all_gather | solution.py:48
  88.2 2.7 fusion.19
  91.0 70.2 %all-gather.13.cloned.1.call-done = bf16[1024,1024]{1,0:T(8,128)(2,1)} async-done(((bf16[64,1024]{1,0:T(8,128)(2,1)}), bf16[1024,1024]{1,0:T(8,128)(2,1)}) %all-gather.13.cloned.1.call-update) | async-done | bytes 2097168 | tf_op jit(solution)/shard_map/all_gather | solution.py:58
  161.2 2.3 fusion.56
  163.8 21.7 %all_to_all.73 = f32[16,1,4096]{2,1,0:T(1,128)S(1)} all-to-all(f32[16,1,4096]{2,1,0:T(1,128)S(1)} %reshape.104), channel_id=1, replica_groups=mesh['tm'=32,'tile'=16] {'tile'}, dimensions={0} | all-to-all | bytes 524288 | tf_op jit(solution)/shard_map/all_to_all | solution.py:62
  189.9 2.5 collective-permute-done
  194.0 69.4 %all-gather.15.cloned.1.call-done = bf16[1024,1024]{1,0:T(8,128)(2,1)} async-done(((bf16[64,1024]{1,0:T(8,128)(2,1)}), bf16[1024,1024]{1,0:T(8,128)(2,1)}) %all-gather.15.cloned.1.call-update) | async-done | bytes 2097168 | tf_op jit(solution)/shard_map/all_gather | solution.py:48
  263.5 2.7 fusion.16
  266.3 70.3 %all-gather.17.cloned.1.call-done = bf16[1024,1024]{1,0:T(8,128)(2,1)} async-done(((bf16[64,1024]{1,0:T(8,128)(2,1)}), bf16[1024,1024]{1,0:T(8,128)(2,1)}) %all-gather.17.cloned.1.call-update) | async-done | bytes 2097168 | tf_op jit(solution)/shard_map/all_gather | solution.py:58
  336.5 2.3 fusion.54
  339.2 21.8 %all_to_all.74 = f32[16,1,4096]{2,1,0:T(1,128)S(1)} all-to-all(f32[16,1,4096]{2,1,0:T(1,128)S(1)} %reshape.106), channel_id=1, replica_groups=mesh['tm'=32,'tile'=16] {'tile'}, dimensions={0} | all-to-all | bytes 524288 | tf_op jit(solution)/shard_map/all_to_all | solution.py:62
  364.8 2.5 collective-permute-done.1
  368.1 69.4 %all-gather.19.cloned.1.call-done = bf16[1024,1024]{1,0:T(8,128)(2,1)} async-done(((bf16[64,1024]{1,0:T(8,128)(2,1)}), bf16[1024,1024]{1,0:T(8,128)(2,1)}) %all-gather.19.cloned.1.call-update) | async-done | bytes 2097168 | tf_op jit(solution)/shard_map/all_gather | solution.py:48
  437.5 2.7 fusion.17
  440.3 70.3 %all-gather.21.cloned.1.call-done = bf16[1024,1024]{1,0:T(8,128)(2,1)} async-done(((bf16[64,1024]{1,0:T(8,128)(2,1)}), bf16[1024,1024]{1,0:T(8,128)(2,1)}) %all-gather.21.cloned.1.call-update) | async-done | bytes 2097168 | tf_op jit(solution)/shard_map/all_gather | solution.py:58
  510.6 2.3 fusion.52
  513.2 21.8 %all_to_all.75 = f32[16,1,4096]{2,1,0:T(1,128)S(1)} all-to-all(f32[16,1,4096]{2,1,0:T(1,128)S(1)} %reshape.108), channel_id=1, replica_groups=mesh['tm'=32,'tile'=16] {'tile'}, dimensions={0} | all-to-all | bytes 524288 | tf_op jit(solution)/shard_map/all_to_all | solution.py:62
  538.9 2.5 collective-permute-done.2
  542.2 69.4 %all-gather.23.cloned.1.call-done = bf16[1024,1024]{1,0:T(8,128)(2,1)} async-done(((bf16[64,1024]{1,0:T(8,128)(2,1)}), bf16[1024,1024]{1,0:T(8,128)(2,1)}) %all-gather.23.cloned.1.call-update) | async-done | bytes 2097168 | tf_op jit(solution)/shard_map/all_gather | solution.py:48
  611.6 2.7 fusion.18
  616.6 30.0 %all-reduce = bf16[1024]{0:T(1024)(128)(2,1)S(1)} all-reduce(bf16[1024]{0:T(1024)(128)(2,1)S(1)} %dynamic-update-slice), channel_id=3, replica_groups=mesh['tm'=32,'tile'=16] {'tile'}, use_global_device_ids=true, to_apply=%add | all-reduce | flops 1024 | bytes 4096 | tf_op jit(solution)/shard_map/all_gather | solution.py:47
  646.7 1.9 collective-permute-start.3
  650.1 27.1 %all-reduce.1 = bf16[1024]{0:T(1024)(128)(2,1)S(1)} all-reduce(bf16[1024]{0:T(1024)(128)(2,1)S(1)} %dynamic-update-slice.1), channel_id=1, replica_groups=mesh['tm'=32,'tile'=16] {'tile'}, use_global_device_ids=true, to_apply=%add.1 | all-reduce | flops 1024 | bytes 4096
  677.4 1.9 collective-permute-start.4
  680.8 29.0 %all-reduce.2 = bf16[1024]{0:T(1024)(128)(2,1)S(1)} all-reduce(bf16[1024]{0:T(1024)(128)(2,1)S(1)} %dynamic-update-slice.2), channel_id=1, replica_groups=mesh['tm'=32,'tile'=16] {'tile'}, use_global_device_ids=true, to_apply=%add.2 | all-reduce | flops 1024 | bytes 4096
  710.0 1.9 collective-permute-start.5
  713.4 27.3 %all-reduce.3 = bf16[1024]{0:T(1024)(128)(2,1)S(1)} all-reduce(bf16[1024]{0:T(1024)(128)(2,1)S(1)} %dynamic-update-slice.3), channel_id=1, replica_groups=mesh['tm'=32,'tile'=16] {'tile'}, use_global_device_ids=true, to_apply=%add.3 | all-reduce | flops 1024 | bytes 4096
  742.5 28.2 %all-gather.2 = f32[16,64,8]{1,2,0:T(8,128)S(1)} all-gather(f32[1,64,8]{1,2,0:T(8,128)S(1)} %bitcast.172), channel_id=1, replica_groups=mesh['tm'=32,'tile'=16] {'tile'}, dimensions={0}, use_global_device_ids=true | all-gather | bytes 34816 | tf_op jit(solution)/shard_map/all_gather | solution.py:83
  772.9 2.4 fusion.50
  776.4 6.6 all-to-all-start.3
  783.0 3.8 fusion
  786.8 30.1 %all-gather.3 = f32[16,64,8]{1,2,0:T(8,128)S(1)} all-gather(f32[1,64,8]{1,2,0:T(8,128)S(1)} %bitcast.173), channel_id=1, replica_groups=mesh['tm'=32,'tile'=16] {'tile'}, dimensions={0}, use_global_device_ids=true | all-gather | bytes 34816 | tf_op jit(solution)/shard_map/all_gather | solution.py:84
  (122 shorter events, 33.0 us)
Async XLA Ops:
  7.2 81.1 %copy-start = (bf16[1,64,1024]{2,1,0:T(8,128)(2,1)S(1)}, bf16[1,64,1024]{2,1,0:T(8,128)(2,1)}, u32[]{:S(2)}) copy-start(bf16[1,64,1024]{2,1,0:T(8,128)(2,1)} %param.12) | copy-start | bytes 393220
  7.2 81.0 %all-gather.27.cloned.1.call-start = ((), (), s32[]{:S(2)}) async-start(), calls=%async_computation.11 | async-start | bytes 2228224 | tf_op jit(solution)/shard_map/all_gather | solution.py:48
  8.8 152.4 %all-gather.13.cloned.1.call-start = ((), (), s32[]{:S(2)}) async-start(), calls=%async_computation.4 | async-start | bytes 2228224 | tf_op jit(solution)/shard_map/all_gather | solution.py:58
  91.0 172.5 %all-gather.15.cloned.1.call-start = ((), (), s32[]{:S(2)}) async-start(), calls=%async_computation.5 | async-start | bytes 2228224 | tf_op jit(solution)/shard_map/all_gather | solution.py:48
  163.5 24.4 %copy-start.2 = (bf16[1,64,1024]{2,1,0:T(8,128)(2,1)S(1)}, bf16[1,64,1024]{2,1,0:T(8,128)(2,1)}, u32[]{:S(2)}) copy-start(bf16[1,64,1024]{2,1,0:T(8,128)(2,1)} %param.14) | copy-start | bytes 393220
  188.0 4.4 collective-permute-start
  194.0 142.6 %all-gather.17.cloned.1.call-start = ((), (), s32[]{:S(2)}) async-start(), calls=%async_computation.6 | async-start | bytes 2228224 | tf_op jit(solution)/shard_map/all_gather | solution.py:58
  266.2 171.3 %all-gather.19.cloned.1.call-start = ((), (), s32[]{:S(2)}) async-start(), calls=%async_computation.7 | async-start | bytes 2228224 | tf_op jit(solution)/shard_map/all_gather | solution.py:48
  339.2 28.2 %copy-start.3 = (bf16[64,1024]{1,0:T(8,128)(2,1)S(1)}, bf16[64,1024]{1,0:T(8,128)(2,1)}, u32[]{:S(2)}) copy-start(bf16[64,1024]{1,0:T(8,128)(2,1)} %bitcast_select_fusion.1) | copy-start | bytes 393220
  362.9 4.4 collective-permute-start.1
  368.0 142.6 %all-gather.21.cloned.1.call-start = ((), (), s32[]{:S(2)}) async-start(), calls=%async_computation.8 | async-start | bytes 2228224 | tf_op jit(solution)/shard_map/all_gather | solution.py:58
  440.3 171.3 %all-gather.23.cloned.1.call-start = ((), (), s32[]{:S(2)}) async-start(), calls=%async_computation.9 | async-start | bytes 2228224 | tf_op jit(solution)/shard_map/all_gather | solution.py:48
  513.2 28.2 %copy-start.4 = (bf16[64,1024]{1,0:T(8,128)(2,1)S(1)}, bf16[64,1024]{1,0:T(8,128)(2,1)}, u32[]{:S(2)}) copy-start(bf16[64,1024]{1,0:T(8,128)(2,1)} %broadcast_select_fusion) | copy-start | bytes 393220
  536.7 79.6 %copy-start.12 = (bf16[8,64]{1,0:T(8,128)(2,1)S(1)}, bf16[8,64]{1,0:T(8,128)(2,1)}, u32[]{:S(2)}) copy-start(bf16[8,64]{1,0:T(8,128)(2,1)} %param.15) | copy-start | bytes 3076
  536.7 109.8 %copy-start.15 = (f32[1,64]{1,0:T(1,128)S(1)}, f32[1,64]{1,0:T(1,128)}, u32[]{:S(2)}) copy-start(f32[1,64]{1,0:T(1,128)} %param.13) | copy-start | bytes 772
  536.9 142.4 %copy-start.14 = (s32[8]{0:T(128)S(1)}, s32[8]{0:T(128)}, u32[]{:S(2)}) copy-start(s32[8]{0:T(128)} %param.21) | copy-start | bytes 100
  536.9 175.0 %copy-start.11 = (s32[8,4]{0,1:T(4,128)S(1)}, s32[8,4]{0,1:T(4,128)}, u32[]{:S(2)}) copy-start(s32[8,4]{0,1:T(4,128)} %param.20) | copy-start | bytes 388
  537.0 4.4 collective-permute-start.2
  542.1 200.4 %copy-start.9 = (f32[8,64]{1,0:T(8,128)S(1)}, f32[8,64]{1,0:T(8,128)}, u32[]{:S(2)}) copy-start(f32[8,64]{1,0:T(8,128)} %param.18) | copy-start | bytes 6148
  542.1 229.4 %copy-start.6 = (f32[8,4,128]{2,1,0:T(4,128)S(1)}, f32[8,4,128]{2,1,0:T(4,128)}, u32[]{:S(2)}) copy-start(f32[8,4,128]{2,1,0:T(4,128)} %param.22) | copy-start | bytes 49156
  542.1 230.8 %all-gather.25.cloned.1.call-start = ((), (), s32[]{:S(2)}) async-start(), calls=%async_computation.10 | async-start | bytes 2228224 | tf_op jit(solution)/shard_map/all_gather | solution.py:58
  646.7 3.2 collective-permute-start.3
  677.4 3.2 collective-permute-start.4
  710.0 3.2 collective-permute-start.5
  742.4 32.9 %copy-start.7 = (f32[8,64]{1,0:T(8,128)}, f32[8,64]{1,0:T(8,128)S(1)}, u32[]{:S(2)}) copy-start(f32[8,64]{1,0:T(8,128)S(1)} %add.74) | copy-start | bytes 6148
  772.9 10.0 %copy-start.1 = (bf16[1,1024,1024]{2,1,0:T(8,128)(2,1)S(1)}, bf16[1,1024,1024]{2,1,0:T(8,128)(2,1)}, u32[]{:S(2)}) copy-start(bf16[1,1024,1024]{2,1,0:T(8,128)(2,1)} %all-gather.27.cloned.1.call-done) | copy-start | bytes 6291460
  776.4 41.5 %all-to-all-start.3 = ((f32[16,1,4096]{2,1,0:T(1,128)}), f32[16,1,4096]{2,1,0:T(1,128)S(1)}, u32[]{:S(2)}, u32[]{:S(2)}) async-start(f32[16,1,4096]{2,1,0:T(1,128)} %reshape.110), calls=%async_computation.3 | async-start | bytes 524288 | tf_op jit(solution)/shard_map/all_to_all | solution.py:62
  783.0 3.8 copy-start.10
  783.0 34.0 %copy-start.13 = (f32[1024]{0:T(1024)S(1)}, f32[1024]{0:T(1024)}, u32[]{:S(2)}) copy-start(f32[1024]{0:T(1024)} %param.23) | copy-start | bytes 12292
  786.8 33.0 %copy-start.5 = (f32[1,64,1024]{2,1,0:T(8,128)S(1)}, f32[1,64,1024]{2,1,0:T(8,128)}, u32[]{:S(2)}) copy-start(f32[1,64,1024]{2,1,0:T(8,128)} %all_to_all.66) | copy-start | bytes 786436
  786.8 33.7 %copy-start.8 = (f32[8,64]{1,0:T(8,128)}, f32[8,64]{1,0:T(8,128)S(1)}, u32[]{:S(2)}) copy-start(f32[8,64]{1,0:T(8,128)S(1)} %add.75) | copy-start | bytes 6148
Sparse Core Ops, SparseCore 0:
  10.7 77.5 all-gather.26
  91.1 70.0 all-gather.12
  194.1 69.3 all-gather.14
  266.3 70.1 all-gather.16
  368.1 69.3 all-gather.18
  440.4 70.1 all-gather.20
  542.2 69.3 all-gather.22
  614.5 70.4 all-gather.24
where the time goes:
time: 828 us; the launch traced here: 827 us
  waiting for transfers between devices  510 us (62%)
  blocking collectives  237 us (29%)
  matrix products  27.8 us (3%)
  starting transfers between devices  18.4 us (2%)
  between operations  15.3 us (2%)
  local copies, waits for them, and re-layouts  10.7 us (1%)
  other arithmetic  8.55 us (1%)
    all_gather x4, waiting for transfers between devices, shards(): lax.all_gather(cur_cov, 'tile', axis=0, tiled=True)  288 us
    all_gather x4, waiting for transfers between devices, shards(): lax.all_gather(product, 'tile', axis=0, tiled=True)  211 us
    unnamed x3, blocking collectives  83.4 us
    all_to_all x3, blocking collectives, shards(): lax.all_to_all(col_block, 'tile', split_axis=0, concat_axis=1, tiled=True)  65.3 us
    all_gather x1, blocking collectives, shards(): lax.all_gather(local_spread, 'tile', axis=1, tiled=True)  30.1 us
    all_gather x1, blocking collectives, shards(): lax.all_gather(cur_mean, 'tile', axis=0, tiled=True)  30 us
    all_gather x1, blocking collectives, shards(): lax.all_gather(local_mean, 'tile', axis=1, tiled=True)  28.2 us
  transfers between devices with their start and end apart: 15, of which 13 were waited for; matrix products, arithmetic and copies ran while one was open for 1% of the time, Pallas kernels for 0%

commit v1 on v0

v1 whole, which is shorter than its diff:
```python
import jax
import jax.numpy as jnp
from jax import lax
from jax.experimental import pallas as pl
from jax.experimental.pallas import tpu as pltpu
from jax.sharding import PartitionSpec as P

MESH = pl.DeviceIdType.MESH
BF16 = jnp.bfloat16
F32 = jnp.float32
N = 1024
RB = 64
T = 128
NT = 8
KEEP = 5
SROWS = KEEP * RB + 16
GA, GB, S0, S1, GC = range(5)


def nn(x, y):
    return jnp.dot(x, y, preferred_element_type=F32)


def nt(x, y):
    return lax.dot_general(x, y, (((1,), (1,)), ((), ())), preferred_element_type=F32)


def mult(i, n):
    return pl.multiple_of(i * n, n)


def kernel(
    gain, off, noise, emean, ecov, sgain, soff, svar, otile, ocount, oval, onoise,
    o_cov, o_mean, o_sm, o_ss, o_in,
    ga, gb, gc, s0, s1, sp, a, x1, x2, d0, d1, dp, ps, rf, acc, xr, mrow, mhop, mb, covbuf, covsend,
    rr, sr, rc, sc, ini_s, ini_r, asem, esem, hop_s, hop_r, fwd_s, fwd_r, mv_s, mv_r, cv_s, cv_r, g_s, g_r,
):
    p = lax.axis_index("tm")
    z = lax.axis_index("tile")
    q = lax.rem(p, 4)
    c = lax.rem(p, 2)
    up = q // 2
    group = p // 4
    core_dev = (p + 1 - 2 * c, z)
    y_dev = (p + 2 - 4 * up, z)
    cross_dev = (p + 3 - 2 * q, z)
    right = (p, lax.rem(z + 1, 16))
    left = (p, lax.rem(z + 15, 16))
    tz = z // 2

    load_a = [
        pltpu.make_async_copy(sgain.at[k], a.at[pl.ds(k * RB, RB), :], asem.at[k]) for k in range(8)
    ]

    bar = pltpu.get_barrier_semaphore()
    for dev in (core_dev, y_dev, cross_dev, right, left):
        pl.semaphore_signal(bar, inc=1, device_id=dev, device_id_type=MESH)

    def ecopy(dd):
        j = mult(lax.rem(tz + dd, NT), T)
        return pltpu.make_async_copy(
            ecov.at[group, :, pl.ds(j, T)], s0.at[z, pl.ds(dd * RB, RB), :], esem.at[dd]
        )

    @pl.when(q == 2)
    def _():
        for dd in range(KEEP):
            ecopy(dd).start()

    def spread_row(row):
        zero = jnp.zeros_like(row)
        even = jnp.concatenate([row, zero], axis=1)
        odd = jnp.concatenate([zero, row], axis=1)
        return jnp.where(lax.rem(z, 2) == 0, even, odd)

    def vector_tile(hi, lo):
        which = lax.broadcasted_iota(jnp.int32, (16, T), 0)
        hi = jnp.broadcast_to(hi, (16, T))
        lo = jnp.broadcast_to(lo, (16, T))
        return jnp.where(which == 0, hi, jnp.where(which == 1, lo, 0.0)).astype(BF16)

    for dd in range(KEEP):
        j = mult(lax.rem(tz + dd, NT), T)
        sp[dd * RB : (dd + 1) * RB, :] = noise[0, :, pl.ds(j, T)]
    off_row = spread_row(off[...])
    off_hi = off_row.astype(BF16).astype(F32)
    sp[KEEP * RB :, :] = vector_tile(off_hi, off_row - off_hi)

    zrow = pl.ds(mult(z, RB), RB)

    @pl.when(c == 1)
    def _():
        ga[zrow, :] = gain[0]

    @pl.when(q == 0)
    def _():
        gc[zrow, :] = gain[0]

    @pl.when(q == 2)
    def _():
        rows = emean[...].astype(F32)
        pick = lax.broadcasted_iota(jnp.int32, rows.shape, 0) == group
        row = spread_row(jnp.sum(jnp.where(pick, rows, 0.0), axis=0, keepdims=True))
        s0[z, KEEP * RB :, :] = vector_tile(row, jnp.zeros_like(row))
        covsend[...] = gain[0]

    pl.semaphore_wait(bar, 5)

    def gat(buf):
        return lambda b: buf.at[pl.ds(mult(b, RB), RB), :]

    def sat(buf):
        return lambda b: buf.at[b]

    def rcopy(src, dst, ssem, rsem, dev):
        return pltpu.make_async_remote_copy(
            src_ref=src, dst_ref=dst, send_sem=ssem, recv_sem=rsem, device_id=dev, device_id_type=MESH
        )

    g2_copy = rcopy(covsend, gb.at[zrow, :], ini_s.at[0], ini_r.at[0], cross_dev)
    n2_copy = rcopy(sp, s1.at[z], ini_s.at[1], ini_r.at[1], y_dev)
    n3_copy = rcopy(sp, s1.at[z], ini_s.at[1], ini_r.at[1], core_dev)
    n1_copy = rcopy(sp, s0.at[z], ini_s.at[1], ini_r.at[2], core_dev)

    @pl.when(q == 3)
    def _():
        n3_copy.start()

    @pl.when(q == 1)
    def _():
        n1_copy.start()

    @pl.when(q == 2)
    def _():
        n2_copy.start()
        g2_copy.start()

    bufs = {GA: gat(ga), GB: gat(gb), S0: sat(s0), S1: sat(s1), GC: gat(gc)}

    def block(o):
        return lax.rem(z - o + 16, 16)

    def ring_send(item, o, ssem, to, dev):
        ref = bufs[item](block(o))
        return rcopy(ref, ref, ssem, rr.at[item, to], dev)

    def core_send(item, o):
        ref = bufs[item](block(o))
        return rcopy(ref, ref, sc.at[item, o], rc.at[item, o], core_dev)

    def ring_recv(item, o):
        ref = bufs[item](block(o))
        rcopy(ref, ref, sr.at[item, 0], rr.at[item, o], right).wait_recv()

    def start(item):
        ring_send(item, 0, sr.at[item, 0], 1, right).start()
        ring_send(item, 0, sr.at[item, 16], 15, left).start()
        if item != GC:
            core_send(item, 0).start()

    def step(item, k):
        ring_recv(item, k)
        ring_send(item, k, sr.at[item, k], k + 1, right).start()
        if item != GC:
            core_send(item, k).start()
        ring_recv(item, 16 - k)

        @pl.when(k < 7)
        def _():
            ring_send(item, 16 - k, sr.at[item, 16 - k], 15 - k, left).start()

        if item != GC:
            core_send(item, 16 - k).start()

    def last(item):
        ring_recv(item, 8)
        if item != GC:
            core_send(item, 8).start()

    def drain(item):
        def body(o, _):
            @pl.when((o != 8) & (o != 9))
            def _():
                ring_send(item, 0, sr.at[item, o], 1, right).wait_send()

            return 0

        lax.fori_loop(0, 17, body, 0)

        if item != GC:

            def body2(o, _):
                core_send(item, o).wait_send()
                return 0

            lax.fori_loop(0, 16, body2, 0)

    def core_recv(item):
        def body(o, _):
            core_send(item, o).wait_recv()
            return 0

        lax.fori_loop(0, 16, body, 0)

    @pl.when(c == 1)
    def _():
        start(GA)

        @pl.when(up == 0)
        def _():
            g2_copy.wait_recv()
            start(GB)

    @pl.when(c == 0)
    def _():
        @pl.when(up == 1)
        def _():
            for dd in range(KEEP):
                ecopy(dd).wait()
            start(S0)
            n3_copy.wait_recv()
            start(S1)

        @pl.when(up == 0)
        def _():
            n1_copy.wait_recv()
            start(S0)
            n2_copy.wait_recv()
            start(S1)
            start(GC)

    for cp in load_a:
        cp.start()

    def loop(k, _):
        @pl.when(c == 1)
        def _():
            step(GA, k)

            @pl.when(up == 0)
            def _():
                step(GB, k)

        @pl.when(c == 0)
        def _():
            step(S0, k)
            step(S1, k)

            @pl.when(up == 0)
            def _():
                step(GC, k)

        return 0

    lax.fori_loop(1, 8, loop, 0)

    @pl.when(c == 1)
    def _():
        last(GA)

        @pl.when(up == 0)
        def _():
            last(GB)

        core_recv(S0)
        core_recv(S1)

    @pl.when(c == 0)
    def _():
        last(S0)
        last(S1)
        core_recv(GA)

        @pl.when(up == 0)
        def _():
            core_recv(GB)

    for cp in load_a:
        cp.wait()

    def put(dense, t, dd, m):
        j = mult(lax.rem(t + dd, NT), T)
        t0 = mult(t, T)
        dense[pl.ds(t0, T), pl.ds(j, T)] = m
        if 1 <= dd <= 3:
            dense[pl.ds(j, T), pl.ds(t0, T)] = m.T

    def stile(s, t, dd):
        return jnp.concatenate(
            [s[2 * t, dd * RB : (dd + 1) * RB, :], s[2 * t + 1, dd * RB : (dd + 1) * RB, :]], axis=0
        )

    def unpack(s, dense):
        def body(t, _):
            for dd in range(KEEP):
                put(dense, t, dd, stile(s, t, dd))
            return 0

        lax.fori_loop(0, NT, body, 0)

    def unpack_state():
        def body(t, _):
            for dd in range(KEEP):
                put(dp, t, dd, ps[t, dd * T : (dd + 1) * T, :])
            return 0

        lax.fori_loop(0, NT, body, 0)

    def mm(x, y, out):
        def body(j, _):
            cols = pl.ds(mult(j, 256), 256)
            out[:, cols] = nn(x[...], y[:, cols]).astype(BF16)
            return 0

        lax.fori_loop(0, 4, body, 0)

    def quad(x, sym):
        def body(j, _):
            cols = pl.ds(mult(j, 256), 256)
            r = nn(x[...], sym[:, cols]) * x[:, cols].astype(F32)
            acc[...] += r[:, :T] + r[:, T:]
            return 0

        lax.fori_loop(0, 4, body, 0)

    def vec(s, row_count):
        parts = []
        for n in range(NT):
            tile = s[2 * n, KEEP * RB :, :].astype(F32) + s[2 * n + 1, KEEP * RB :, :].astype(F32)
            parts.append(tile)
        whole = jnp.concatenate(parts, axis=1)
        return whole[0:1, :] + whole[1:2, :] if row_count == 2 else whole[0:1, :]

    def set_mean(row):
        mrow[...] = jnp.broadcast_to(row, (16, N)).astype(BF16)

    def apply_mean(g, s):
        set_mean(nt(mrow[...], g[...])[0:1, :] + vec(s, 2))

    def step_means():
        r = nt(mrow[...], a[...])
        for k in range(8):
            o_sm[k : k + 1, :] = r[0:1, k * RB : (k + 1) * RB] + soff[k : k + 1, :]

    def own_mean():
        o_mean[...] = nt(mrow[...], gain[0])[0:1, :] + off[...]

    def finish_spread():
        row = jnp.sum(acc[...].T, axis=0, keepdims=True)
        for k in range(8):
            o_ss[k : k + 1, :] = row[:, k * RB : (k + 1) * RB] + svar[k : k + 1, :]

    def gather_copy(o):
        return rcopy(mb.at[z], mb.at[z], g_s.at[o], g_r.at[o], (p, lax.rem(z + o, 16)))

    def send_moments():
        mb[z] = jnp.concatenate([spread_row(o_sm[...]), spread_row(o_ss[...])], axis=0)

        def body(i, _):
            gather_copy(lax.rem(i + 7, 15) + 1).start()
            return 0

        lax.fori_loop(0, 15, body, 0)

    def hop_copy(t):
        return rcopy(ps.at[t], ps.at[t], hop_s.at[t], hop_r.at[t], y_dev)

    def fwd_copy(t):
        return rcopy(ps.at[t], ps.at[t], fwd_s.at[t], fwd_r.at[t], core_dev)

    mean_hop = rcopy(mrow, mhop, mv_s.at[0], mv_r.at[0], y_dev)
    cov_hop = rcopy(covsend, covbuf, cv_s.at[0], cv_r.at[0], cross_dev)
    other = (1 - c) * 4

    acc[...] = jnp.zeros_like(acc)

    @pl.when(up == 1)
    def _():
        unpack(s0, d0)
        half = pl.ds(mult(c, 512), 512)
        mm(ga.at[half, :], d0, x1)

        def body(i, _):
            t = c * 4 + i
            w = x1[pl.ds(mult(i, T), T), :]
            rf[...] = nt(w, ga[...])
            for dd in range(KEEP):
                j = mult(lax.rem(t + dd, NT), T)
                m = rf[:, pl.ds(j, T)] + stile(s1, t, dd).astype(F32)
                ps[t, dd * T : (dd + 1) * T, :] = m.astype(BF16)
            hop_copy(t).start()

            @pl.when(c == 1)
            def _():
                fwd_copy(t).start()

            return 0

        lax.fori_loop(0, 4, body, 0)
        set_mean(vec(s0, 1))

        @pl.when(q == 3)
        def _():
            step_means()
            own_mean()

        apply_mean(ga, s1)
        mean_hop.start()

        @pl.when(q == 3)
        def _():
            quad(a, d0)
            finish_spread()
            send_moments()
            mm(gain.at[0], d0, xr)
            o_cov[0] = (nt(xr[...], ga[...]) + noise[0].astype(F32)).astype(BF16)

        @pl.when(q == 2)
        def _():
            def rbody(i, _):
                fwd_copy(4 + i).wait_recv()
                return 0

            lax.fori_loop(0, 4, rbody, 0)
            unpack_state()
            step_means()
            own_mean()
            quad(a, dp)
            finish_spread()
            send_moments()
            cov_hop.wait_recv()
            o_cov[0] = covbuf[...]

    @pl.when(up == 0)
    def _():
        unpack(s1, d1)

        @pl.when(q == 1)
        def _():
            mm(a, gb, x1)
            quad(a, d1)

        @pl.when(q == 0)
        def _():
            unpack(s0, d0)
            mm(a, ga, x2)
            quad(a, d0)
            quad(x2, d1)
            mm(x2, gb, x1)

        def fbody(i, _):
            t = c * 4 + i
            hop_copy(t).wait_recv()
            fwd_copy(t).start()
            return 0

        lax.fori_loop(0, 4, fbody, 0)

        def gbody(i, _):
            fwd_copy(other + i).wait_recv()
            return 0

        lax.fori_loop(0, 4, gbody, 0)
        mean_hop.wait_recv()
        unpack_state()
        quad(x1, dp)
        finish_spread()
        mrow[...] = mhop[...]
        apply_mean(gb, s1)

        @pl.when(q == 0)
        def _():
            apply_mean(ga, s0)

        step_means()
        send_moments()
        own_mean()

        @pl.when(q == 1)
        def _():
            mm(gb.at[zrow, :], dp, xr)
            covsend[...] = (nt(xr[...], gb[...]) + d1[zrow, :].astype(F32)).astype(BF16)
            cov_hop.start()
            mm(gain.at[0], gb, xr)
            covbuf[...] = nn(xr[...], dp[...]).astype(BF16)
            xr[...] = (nt(covbuf[...], gb[...]) + nn(gain[0], d1[...])).astype(BF16)
            o_cov[0] = (nt(xr[...], ga[...]) + noise[0].astype(F32)).astype(BF16)
            cov_hop.wait_send()

        @pl.when(q == 0)
        def _():
            last(GC)
            mm(gain.at[0], ga, xr)
            mm(xr, gb, covbuf)
            covsend[...] = nn(covbuf[...], dp[...]).astype(BF16)
            covbuf[...] = (nt(covsend[...], gb[...]) + nn(xr[...], d1[...])).astype(BF16)
            xr[...] = (nt(covbuf[...], ga[...]) + nn(gain[0], d0[...])).astype(BF16)
            o_cov[0] = (nt(xr[...], gc[...]) + noise[0].astype(F32)).astype(BF16)

    @pl.when(c == 1)
    def _():
        drain(GA)
        n3_copy.wait_send()

        @pl.when(up == 0)
        def _():
            drain(GB)

    @pl.when(c == 0)
    def _():
        drain(S0)
        drain(S1)

        @pl.when(up == 0)
        def _():
            drain(GC)

    @pl.when(q == 2)
    def _():
        n2_copy.wait_send()
        g2_copy.wait_send()

    def sbody(i, _):
        t = c * 4 + i

        @pl.when(up == 1)
        def _():
            hop_copy(t).wait_send()

        @pl.when(q != 2)
        def _():
            fwd_copy(t).wait_send()

        return 0

    lax.fori_loop(0, 4, sbody, 0)

    @pl.when(up == 1)
    def _():
        mean_hop.wait_send()

    def wbody(o, _):
        ref = mb.at[block(o)]
        rcopy(ref, ref, g_s.at[o], g_r.at[o], right).wait_recv()
        return 0

    lax.fori_loop(1, 16, wbody, 0)
    picked_mean = [jnp.zeros((8, T), F32) for _ in range(4)]
    picked_spread = [jnp.zeros((8, T), F32) for _ in range(4)]
    for n in range(NT):
        tile = mb[2 * n] + mb[2 * n + 1]
        mean_n = tile[:8, :]
        spread_n = tile[8:, :] + onoise[n : n + 1, :]
        for j in range(4):
            hit = otile[:, j : j + 1] == n
            picked_mean[j] = jnp.where(hit, mean_n, picked_mean[j])
            picked_spread[j] = jnp.where(hit, spread_n, picked_spread[j])
    for j in range(4):
        value = (oval[:, j, :] - picked_mean[j]) / picked_spread[j]
        o_in[:, j, :] = jnp.where(ocount[...] > j, value, 0.0)

    def vbody(o, _):
        gather_copy(o).wait_send()
        return 0

    lax.fori_loop(1, 16, vbody, 0)


def shards(
    seg_gain, seg_offset, seg_noise, end_mean, end_cov, step_gain,
    step_offset, step_var, obs_tiles, obs_count, obs_value, obs_noise,
):
    vmem = pl.BlockSpec(memory_space=pltpu.VMEM)
    hbm = pl.BlockSpec(memory_space=pl.ANY)
    dma = pltpu.SemaphoreType.DMA
    out_cov, out_mean, step_mean, step_spread, innovation = pl.pallas_call(
        kernel,
        out_shape=(
            jax.ShapeDtypeStruct((1, RB, N), BF16),
            jax.ShapeDtypeStruct((1, RB), F32),
            jax.ShapeDtypeStruct((8, RB), F32),
            jax.ShapeDtypeStruct((8, RB), F32),
            jax.ShapeDtypeStruct((8, 4, T), F32),
        ),
        in_specs=[vmem, vmem, vmem, vmem, hbm, hbm, vmem, vmem, vmem, vmem, vmem, vmem],
        out_specs=(vmem,) * 5,
        scratch_shapes=[
            pltpu.VMEM((N, N), BF16),
            pltpu.VMEM((N, N), BF16),
            pltpu.VMEM((N, N), BF16),
            pltpu.VMEM((16, SROWS, T), BF16),
            pltpu.VMEM((16, SROWS, T), BF16),
            pltpu.VMEM((SROWS, T), BF16),
            pltpu.VMEM((512, N), BF16),
            pltpu.VMEM((512, N), BF16),
            pltpu.VMEM((512, N), BF16),
            pltpu.VMEM((N, N), BF16),
            pltpu.VMEM((N, N), BF16),
            pltpu.VMEM((N, N), BF16),
            pltpu.VMEM((NT, KEEP * T, T), BF16),
            pltpu.VMEM((T, N), F32),
            pltpu.VMEM((512, T), F32),
            pltpu.VMEM((RB, N), BF16),
            pltpu.VMEM((16, N), BF16),
            pltpu.VMEM((16, N), BF16),
            pltpu.VMEM((16, 16, T), F32),
            pltpu.VMEM((RB, N), BF16),
            pltpu.VMEM((RB, N), BF16),
            dma((5, 16)), dma((5, 17)), dma((5, 16)), dma((5, 16)),
            dma((2,)), dma((3,)), dma((8,)), dma((KEEP,)),
            dma((8,)), dma((8,)), dma((8,)), dma((8,)),
            dma((1,)), dma((1,)), dma((1,)), dma((1,)),
            dma((16,)), dma((16,)),
        ],
        compiler_params=pltpu.CompilerParams(
            collective_id=0, has_side_effects=True, vmem_limit_bytes=48 * 2**20
        ),
    )(
        seg_gain, seg_offset, seg_noise, end_mean, end_cov, step_gain,
        step_offset, step_var, obs_tiles, obs_count.reshape(8, 1), obs_value, obs_noise.reshape(NT, T),
    )
    return out_cov, out_mean.astype(BF16), step_mean, step_spread, innovation


def solution(mesh):
    in_specs = (
        P("tm", "tile", None), P("tm", "tile"), P("tm", "tile", None), P(None, "tile"),
        P(None, "tile", None), P("tm", "tile", None), P("tm", "tile"), P("tm", "tile"),
        P("tm", None), P("tm"), P("tm", None, None), P(),
    )
    out_specs = (
        P("tm", "tile", None), P("tm", "tile"), P("tm", "tile"), P("tm", "tile"), P("tm", None, None),
    )
    return jax.shard_map(shards, mesh=mesh, in_specs=in_specs, out_specs=out_specs, check_vma=False)
```

time: 828 us -> 102 us (0.12)
  the two profiles are of different devices: /device:TPU:4 before, /device:TPU:1 now
where the time goes in v1:
time: 102 us
  Pallas kernels  90.8 us (89%)
  local copies, waits for them, and re-layouts  9.59 us (9%)
    pallas_call x1, Pallas kernels, shards(): pl.pallas_call(kernel, out_shape=(jax.ShapeDtypeStruct((1, RB, N), BF16),...  90.8 us
    unnamed x25, local copies, waits for them, and re-layouts  8.86 us

profile of v1, /device:TPU:1, one launch (start us, length us, event | category | flops | bytes accessed | tf_op | source)
XLA Modules:
  0.0 101.6 jit_solution(2194641905738022062)
XLA Ops:
  0.6 0.0 copy-start.8
  0.6 0.0 copy-start.7
  0.7 0.0 copy-start.5
  0.7 0.0 copy-start.6
  0.7 0.8 copy.17.otile
  1.5 0.7 copy.18.ocount
  2.2 0.0 copy-done.8
  2.2 0.0 copy-done.7
  2.2 0.0 copy-done.5
  2.2 0.0 copy-done.6
  2.2 0.0 copy-start
  2.2 1.2 %copy-done = bf16[8,64,1024]{2,1,0:T(8,128)(2,1)S(1)} copy-done((bf16[8,64,1024]{2,1,0:T(8,128)(2,1)S(1)}, bf16[8,64,1024]{2,1,0:T(8,128)(2,1)}, u32[]{:S(2)}) %copy-start) | copy-done | bytes 1048600
  3.4 0.0 copy-start.1
  3.4 1.2 %copy-done.1 = bf16[8,64,1024]{2,1,0:T(8,128)(2,1)S(1)} copy-done((bf16[8,64,1024]{2,1,0:T(8,128)(2,1)S(1)}, bf16[8,64,1024]{2,1,0:T(8,128)(2,1)}, u32[]{:S(2)}) %copy-start.1) | copy-done | bytes 1048600
  4.6 0.0 copy-start.2
  4.7 0.9 copy-done.2
  5.6 0.0 copy-start.3
  5.6 0.9 copy-done.3
  6.5 0.0 copy-start.4
  6.5 0.7 copy-done.4
  7.2 0.0 copy-start.9
  7.2 0.7 copy-done.9
  7.8 90.8 %shard_map.155 = (bf16[1,64,1024]{2,1,0:T(8,128)(2,1)S(1)}, f32[1,64]{1,0:T(1,128)S(1)}, f32[8,64]{1,0:T(8,128)S(1)}, f32[8,64]{1,0:T(8,128)S(1)}, f32[8,4,128]{2,1,0:T(4,128)S(1)}) custom-call(bf16[1,64,1024]{2,1,0:T(8,128)(2,1)S(1)} %copy-done.2, f32[1,64]{1,0:T(1,128)S(1)} %copy-done.9, bf16[1,64,1024]{2,1,0:T(8,128)(2,1)S(1)} %copy-done.3, ...), custom_call_target="tpu_custom_call" | custom-call | tf_op jit(solution)/shard_map/pallas_call | solution.py:576
  98.6 0.5 convert_element_type.3
  99.1 0.7 copy.23
  99.8 0.6 copy.24
  100.4 0.6 copy.25
  101.0 0.6 copy.26
Async XLA Ops:
  0.6 1.6 %copy-start.8 = (bf16[8,64]{1,0:T(8,128)(2,1)S(1)}, bf16[8,64]{1,0:T(8,128)(2,1)}, u32[]{:S(2)}) copy-start(bf16[8,64]{1,0:T(8,128)(2,1)} %emean.1) | copy-start | bytes 3076
  0.6 1.5 %copy-start.7 = (f32[1024]{0:T(1024)S(1)}, f32[1024]{0:T(1024)}, u32[]{:S(2)}) copy-start(f32[1024]{0:T(1024)} %param.23) | copy-start | bytes 12292
  0.7 1.5 %copy-start.5 = (f32[8,64]{1,0:T(8,128)S(1)}, f32[8,64]{1,0:T(8,128)}, u32[]{:S(2)}) copy-start(f32[8,64]{1,0:T(8,128)} %soff.1) | copy-start | bytes 6148
  0.7 1.5 %copy-start.6 = (f32[8,64]{1,0:T(8,128)S(1)}, f32[8,64]{1,0:T(8,128)}, u32[]{:S(2)}) copy-start(f32[8,64]{1,0:T(8,128)} %svar.1) | copy-start | bytes 6148
  2.2 1.2 %copy-start = (bf16[8,64,1024]{2,1,0:T(8,128)(2,1)S(1)}, bf16[8,64,1024]{2,1,0:T(8,128)(2,1)}, u32[]{:S(2)}) copy-start(bf16[8,64,1024]{2,1,0:T(8,128)(2,1)} %ecov.1) | copy-start | bytes 3145732
  3.4 1.2 %copy-start.1 = (bf16[8,64,1024]{2,1,0:T(8,128)(2,1)S(1)}, bf16[8,64,1024]{2,1,0:T(8,128)(2,1)}, u32[]{:S(2)}) copy-start(bf16[8,64,1024]{2,1,0:T(8,128)(2,1)} %sgain.1) | copy-start | bytes 3145732
  4.6 0.9 copy-start.2
  5.6 0.9 copy-start.3
  6.5 0.7 copy-start.4
  7.2 0.7 copy-start.9

commit v2 on v1

--- a/solution.py
+++ b/solution.py
@@ -14,7 +14,15 @@
 NT = 8
 KEEP = 5
 SROWS = KEEP * RB + 16
-GA, GB, S0, S1, GC = range(5)
+GA, GB, GC, S0, S1 = range(5)
+CG = 2
+CS = 2
+NPARTS = 3 * CG + 2 * CS
+PARTS = {i: tuple(range(i * CG, (i + 1) * CG)) for i in (GA, GB, GC)}
+PARTS |= {i: tuple(range(3 * CG + (i - S0) * CS, 3 * CG + (i - S0 + 1) * CS)) for i in (S0, S1)}
+S_CUTS = {1: ((0, SROWS),), 2: ((0, 176), (176, 160))}[CS]
+LAG_B = 1
+LAG_C = 2
 
 
 def nn(x, y):
@@ -30,9 +38,10 @@
 
 
 def kernel(
-    gain, off, noise, emean, ecov, sgain, soff, svar, otile, ocount, oval, onoise,
+    gain_h, off_h, noise_h, emean_h, ecov, sgain, soff_h, svar_h, otile_h, ocount_h, oval_h, onoise_h,
     o_cov, o_mean, o_sm, o_ss, o_in,
-    ga, gb, gc, s0, s1, sp, a, x1, x2, d0, d1, dp, ps, rf, acc, xr, mrow, mhop, mb, covbuf, covsend,
+    ga, gb, gc, s0, s1, sp, a, x1, x2, d0, d1, dp, ps, rf, acc, mpre, xr, mrow, mhop, mb, covbuf, covsend,
+    gain, off, noise, emean, soff, svar, otile, ocount, oval, onoise, lsem,
     rr, sr, rc, sc, ini_s, ini_r, asem, esem, hop_s, hop_r, fwd_s, fwd_r, mv_s, mv_r, cv_s, cv_r, g_s, g_r,
 ):
     p = lax.axis_index("tm")
@@ -52,6 +61,12 @@
         pltpu.make_async_copy(sgain.at[k], a.at[pl.ds(k * RB, RB), :], asem.at[k]) for k in range(8)
     ]
 
+    pairs = (
+        (gain_h, gain), (noise_h, noise), (off_h, off), (emean_h, emean), (soff_h, soff),
+        (svar_h, svar), (otile_h, otile), (ocount_h, ocount), (oval_h, oval), (onoise_h, onoise),
+    )
+    loads = [pltpu.make_async_copy(src, dst, lsem.at[i]) for i, (src, dst) in enumerate(pairs)]
+
     bar = pltpu.get_barrier_semaphore()
     for dev in (core_dev, y_dev, cross_dev, right, left):
         pl.semaphore_signal(bar, inc=1, device_id=dev, device_id_type=MESH)
@@ -66,6 +81,13 @@
     def _():
         for dd in range(KEEP):
             ecopy(dd).start()
+
+    for cp in loads:
+        cp.start()
+    for cp in load_a:
+        cp.start()
+    for cp in loads[:4]:
+        cp.wait()
 
     def spread_row(row):
         zero = jnp.zeros_like(row)
@@ -92,10 +114,6 @@
     def _():
         ga[zrow, :] = gain[0]
 
-    @pl.when(q == 0)
-    def _():
-        gc[zrow, :] = gain[0]
-
     @pl.when(q == 2)
     def _():
         rows = emean[...].astype(F32)
@@ -121,6 +139,7 @@
     n2_copy = rcopy(sp, s1.at[z], ini_s.at[1], ini_r.at[1], y_dev)
     n3_copy = rcopy(sp, s1.at[z], ini_s.at[1], ini_r.at[1], core_dev)
     n1_copy = rcopy(sp, s0.at[z], ini_s.at[1], ini_r.at[2], core_dev)
+    g0_copy = rcopy(gain.at[0], gc.at[zrow, :], ini_s.at[0], ini_r.at[1], core_dev)
 
     @pl.when(q == 3)
     def _():
@@ -129,71 +148,84 @@
     @pl.when(q == 1)
     def _():
         n1_copy.start()
+
+    @pl.when(q == 0)
+    def _():
+        g0_copy.start()
 
     @pl.when(q == 2)
     def _():
         n2_copy.start()
         g2_copy.start()
 
-    bufs = {GA: gat(ga), GB: gat(gb), S0: sat(s0), S1: sat(s1), GC: gat(gc)}
+    whole = {GA: gat(ga), GB: gat(gb), GC: gat(gc), S0: sat(s0), S1: sat(s1)}
+
+    def piece(buf, i):
+        rows = RB // CG
+        return lambda b: buf.at[pl.ds(pl.multiple_of(b * RB + i * rows, rows), rows), :]
+
+    def spiece(buf, i):
+        return lambda b: buf.at[b, pl.ds(*S_CUTS[i]), :]
+
+    bufs = [piece(g, i) for g in (ga, gb, gc) for i in range(CG)]
+    bufs += [spiece(s, i) for s in (s0, s1) for i in range(CS)]
 
     def block(o):
         return lax.rem(z - o + 16, 16)
 
-    def ring_send(item, o, ssem, to, dev):
-        ref = bufs[item](block(o))
-        return rcopy(ref, ref, ssem, rr.at[item, to], dev)
+    def ring_send(part, o, ssem, to, dev):
+        ref = bufs[part](block(o))
+        return rcopy(ref, ref, ssem, rr.at[part, to], dev)
 
     def core_send(item, o):
-        ref = bufs[item](block(o))
+        ref = whole[item](block(o))
         return rcopy(ref, ref, sc.at[item, o], rc.at[item, o], core_dev)
 
-    def ring_recv(item, o):
-        ref = bufs[item](block(o))
-        rcopy(ref, ref, sr.at[item, 0], rr.at[item, o], right).wait_recv()
+    def ring_recv(part, o):
+        ref = bufs[part](block(o))
+        rcopy(ref, ref, sr.at[part, 0], rr.at[part, o], right).wait_recv()
 
     def start(item):
-        ring_send(item, 0, sr.at[item, 0], 1, right).start()
-        ring_send(item, 0, sr.at[item, 16], 15, left).start()
-        if item != GC:
-            core_send(item, 0).start()
+        for part in PARTS[item]:
+            ring_send(part, 0, sr.at[part, 0], 1, right).start()
+            ring_send(part, 0, sr.at[part, 16], 15, left).start()
+        core_send(item, 0).start()
 
     def step(item, k):
-        ring_recv(item, k)
-        ring_send(item, k, sr.at[item, k], k + 1, right).start()
-        if item != GC:
-            core_send(item, k).start()
-        ring_recv(item, 16 - k)
-
-        @pl.when(k < 7)
-        def _():
-            ring_send(item, 16 - k, sr.at[item, 16 - k], 15 - k, left).start()
-
-        if item != GC:
-            core_send(item, 16 - k).start()
+        for part in PARTS[item]:
+            ring_recv(part, k)
+            ring_send(part, k, sr.at[part, k], k + 1, right).start()
+            ring_recv(part, 16 - k)
+
+            @pl.when(k < 7)
+            def _():
+                ring_send(part, 16 - k, sr.at[part, 16 - k], 15 - k, left).start()
+
+        core_send(item, k).start()
+        core_send(item, 16 - k).start()
 
     def last(item):
-        ring_recv(item, 8)
-        if item != GC:
-            core_send(item, 8).start()
+        for part in PARTS[item]:
+            ring_recv(part, 8)
+        core_send(item, 8).start()
 
     def drain(item):
-        def body(o, _):
-            @pl.when((o != 8) & (o != 9))
-            def _():
-                ring_send(item, 0, sr.at[item, o], 1, right).wait_send()
-
-            return 0
-
-        lax.fori_loop(0, 17, body, 0)
-
-        if item != GC:
-
-            def body2(o, _):
-                core_send(item, o).wait_send()
+        for part in PARTS[item]:
+
+            def body(o, _):
+                @pl.when((o != 8) & (o != 9))
+                def _():
+                    ring_send(part, 0, sr.at[part, o], 1, right).wait_send()
+
                 return 0
 
-            lax.fori_loop(0, 16, body2, 0)
+            lax.fori_loop(0, 17, body, 0)
+
+        def body2(o, _):
+            core_send(item, o).wait_send()
+            return 0
+
+        lax.fori_loop(0, 16, body2, 0)
 
     def core_recv(item):
         def body(o, _):
@@ -202,79 +234,59 @@
 
         lax.fori_loop(0, 16, body, 0)
 
-    @pl.when(c == 1)
+    def steps(lo, hi, *items):
+        def body(k, _):
+            for item, lag in items:
+                step(item, k - lag)
+            return 0
+
+        lax.fori_loop(lo, hi, body, 0)
+
+    @pl.when(q == 3)
     def _():
         start(GA)
-
-        @pl.when(up == 0)
-        def _():
-            g2_copy.wait_recv()
-            start(GB)
-
-    @pl.when(c == 0)
-    def _():
-        @pl.when(up == 1)
-        def _():
-            for dd in range(KEEP):
-                ecopy(dd).wait()
-            start(S0)
-            n3_copy.wait_recv()
-            start(S1)
-
-        @pl.when(up == 0)
-        def _():
-            n1_copy.wait_recv()
-            start(S0)
-            n2_copy.wait_recv()
-            start(S1)
-            start(GC)
-
-    for cp in load_a:
-        cp.start()
-
-    def loop(k, _):
-        @pl.when(c == 1)
-        def _():
-            step(GA, k)
-
-            @pl.when(up == 0)
-            def _():
-                step(GB, k)
-
-        @pl.when(c == 0)
-        def _():
-            step(S0, k)
-            step(S1, k)
-
-            @pl.when(up == 0)
-            def _():
-                step(GC, k)
-
-        return 0
-
-    lax.fori_loop(1, 8, loop, 0)
-
-    @pl.when(c == 1)
-    def _():
+        steps(1, 8, (GA, 0))
         last(GA)
 
-        @pl.when(up == 0)
-        def _():
-            last(GB)
-
-        core_recv(S0)
-        core_recv(S1)
-
-    @pl.when(c == 0)
-    def _():
+    @pl.when(q == 2)
+    def _():
+        for dd in range(KEEP):
+            ecopy(dd).wait()
+        start(S0)
+        n3_copy.wait_recv()
+        start(S1)
+        steps(1, 8, (S0, 0), (S1, 0))
         last(S0)
         last(S1)
-        core_recv(GA)
-
-        @pl.when(up == 0)
-        def _():
-            core_recv(GB)
-
+
+    @pl.when(q == 1)
+    def _():
+        start(GA)
+        steps(1, 1 + LAG_B, (GA, 0))
+        g2_copy.wait_recv()
+        start(GB)
+        g0_copy.wait_recv()
+        steps(1 + LAG_B, 1 + LAG_C, (GA, 0), (GB, LAG_B))
+        start(GC)
+        steps(1 + LAG_C, 8, (GA, 0), (GB, LAG_B), (GC, LAG_C))
+        last(GA)
+        steps(8, 8 + LAG_B, (GB, LAG_B), (GC, LAG_C))
+        last(GB)
+
+    @pl.when(q == 0)
+    def _():
+        n1_copy.wait_recv()
+        start(S0)
+        steps(1, 1 + LAG_B, (S0, 0))
+        n2_copy.wait_recv()
+        start(S1)
+        steps(1 + LAG_B, 8, (S0, 0), (S1, LAG_B))
+        last(S0)
+        steps(8, 8 + LAG_B, (S1, LAG_B))
+        last(S1)
+
+    for cp in loads[4:]:
+        cp.wait()
     for cp in load_a:
         cp.wait()
 
@@ -298,30 +310,40 @@
 
         lax.fori_loop(0, NT, body, 0)
 
-    def unpack_state():
-        def body(t, _):
-            for dd in range(KEEP):
-                put(dp, t, dd, ps[t, dd * T : (dd + 1) * T, :])
-            return 0
-
-        lax.fori_loop(0, NT, body, 0)
+    def put_state(t):
+        for dd in range(KEEP):
+            put(dp, t, dd, ps[t, dd * T : (dd + 1) * T, :])
+
+    def mm_cols(x, y, out, j):
+        cols = pl.ds(mult(j, 256), 256)
+        out[:, cols] = nn(x[...], y[:, cols]).astype(BF16)
+
+    def quad_cols(x, sym, j):
+        cols = pl.ds(mult(j, 256), 256)
+        r = nn(x[...], sym[:, cols]) * x[:, cols].astype(F32)
+        acc[...] += r[:, :T] + r[:, T:]
 
     def mm(x, y, out):
         def body(j, _):
-            cols = pl.ds(mult(j, 256), 256)
-            out[:, cols] = nn(x[...], y[:, cols]).astype(BF16)
+            mm_cols(x, y, out, j)
             return 0
 
         lax.fori_loop(0, 4, body, 0)
 
     def quad(x, sym):
         def body(j, _):
-            cols = pl.ds(mult(j, 256), 256)
-            r = nn(x[...], sym[:, cols]) * x[:, cols].astype(F32)
-            acc[...] += r[:, :T] + r[:, T:]
+            quad_cols(x, sym, j)
             return 0
 
         lax.fori_loop(0, 4, body, 0)
+
+    def vec_rows(s):
+        parts = [s[2 * n, KEEP * RB :, :].astype(F32) + s[2 * n + 1, KEEP * RB :, :].astype(F32) for n in range(NT)]
+        return jnp.concatenate(parts, axis=1).astype(BF16)
+
+    def offset_part(s, x):
+        r = nt(vec_rows(s), x[...])
+        return r[0:1, :] + r[1:2, :]
 
     def vec(s, row_count):
         parts = []
@@ -337,10 +359,12 @@
     def apply_mean(g, s):
         set_mean(nt(mrow[...], g[...])[0:1, :] + vec(s, 2))
 
-    def step_means():
-        r = nt(mrow[...], a[...])
+    def put_means(r):
         for k in range(8):
             o_sm[k : k + 1, :] = r[0:1, k * RB : (k + 1) * RB] + soff[k : k + 1, :]
+
+    def step_means():
+        put_means(nt(mrow[...], a[...])[0:1, :])
 
     def own_mean():
         o_mean[...] = nt(mrow[...], gain[0])[0:1, :] + off[...]
@@ -376,9 +400,22 @@
 
     @pl.when(up == 1)
     def _():
+        @pl.when(c == 1)
+        def _():
+            core_recv(S0)
+
         unpack(s0, d0)
-        half = pl.ds(mult(c, 512), 512)
-        mm(ga.at[half, :], d0, x1)
+
+        @pl.when(c == 0)
+        def _():
+            core_recv(GA)
+
+        own_half = pl.ds(mult(c, 512), 512)
+        mm(ga.at[own_half, :], d0, x1)
+
+        @pl.when(c == 1)
+        def _():
+            core_recv(S1)
 
         def body(i, _):
             t = c * 4 + i
@@ -418,11 +455,12 @@
         @pl.when(q == 2)
         def _():
             def rbody(i, _):
+                put_state(i)
                 fwd_copy(4 + i).wait_recv()
+                put_state(4 + i)
                 return 0
 
             lax.fori_loop(0, 4, rbody, 0)
-            unpack_state()
             step_means()
             own_mean()
             quad(a, dp)
@@ -433,38 +471,61 @@
 
     @pl.when(up == 0)
     def _():
-        unpack(s1, d1)
-
         @pl.when(q == 1)
         def _():
-            mm(a, gb, x1)
-            quad(a, d1)
+            core_recv(S0)
+            core_recv(S1)
+            step(GC, 8 - LAG_C + LAG_B)
+            unpack(s1, d1)
+
+            def work(j, _):
+                mm_cols(a, gb, x1, j)
+                quad_cols(a, d1, j)
+
+                @pl.when(j < LAG_C - LAG_B - 1)
+                def _():
+                    step(GC, 9 - LAG_C + LAG_B + j)
+
+                return 0
+
+            lax.fori_loop(0, 4, work, 0)
+            last(GC)
+            mpre[...] = offset_part(s1, a)
 
         @pl.when(q == 0)
         def _():
             unpack(s0, d0)
+            core_recv(GA)
             mm(a, ga, x2)
             quad(a, d0)
+            unpack(s1, d1)
             quad(x2, d1)
+            core_recv(GB)
             mm(x2, gb, x1)
+            mpre[...] = offset_part(s0, a) + offset_part(s1, x2)
+            mm(gain.at[0], ga, xr)
+            mm(xr, gb, covbuf)
 
         def fbody(i, _):
             t = c * 4 + i
             hop_copy(t).wait_recv()
             fwd_copy(t).start()
+            put_state(t)
             return 0
 
         lax.fori_loop(0, 4, fbody, 0)
 
         def gbody(i, _):
             fwd_copy(other + i).wait_recv()
+            put_state(other + i)
             return 0
 
         lax.fori_loop(0, 4, gbody, 0)
-        mean_hop.wait_recv()
-        unpack_state()
         quad(x1, dp)
         finish_spread()
+        mean_hop.wait_recv()
+        put_means(nt(mhop[...], x1[...])[0:1, :] + mpre[...])
+        send_moments()
         mrow[...] = mhop[...]
         apply_mean(gb, s1)
 
@@ -472,8 +533,6 @@
         def _():
             apply_mean(ga, s0)
 
-        step_means()
-        send_moments()
         own_mean()
 
         @pl.when(q == 1)
@@ -489,12 +548,10 @@
 
         @pl.when(q == 0)
         def _():
-            last(GC)
-            mm(gain.at[0], ga, xr)
-            mm(xr, gb, covbuf)
             covsend[...] = nn(covbuf[...], dp[...]).astype(BF16)
             covbuf[...] = (nt(covsend[...], gb[...]) + nn(xr[...], d1[...])).astype(BF16)
             xr[...] = (nt(covbuf[...], ga[...]) + nn(gain[0], d0[...])).astype(BF16)
+            core_recv(GC)
             o_cov[0] = (nt(xr[...], gc[...]) + noise[0].astype(F32)).astype(BF16)
 
     @pl.when(c == 1)
@@ -505,6 +562,7 @@
         @pl.when(up == 0)
         def _():
             drain(GB)
+            drain(GC)
 
     @pl.when(c == 0)
     def _():
@@ -513,7 +571,7 @@
 
         @pl.when(up == 0)
         def _():
-            drain(GC)
+            g0_copy.wait_send()
 
     @pl.when(q == 2)
     def _():
@@ -545,6 +603,13 @@
         return 0
 
     lax.fori_loop(1, 16, wbody, 0)
+    eye = lax.broadcasted_iota(jnp.int32, (8, 8), 0) == lax.broadcasted_iota(jnp.int32, (8, 8), 1)
+
+    def column(row):
+        return jnp.sum(jnp.where(eye, row.astype(F32), 0.0), axis=1, keepdims=True)
+
+    tiles = [column(otile[j : j + 1, :]) for j in range(4)]
+    counts = column(ocount[...])
     picked_mean = [jnp.zeros((8, T), F32) for _ in range(4)]
     picked_spread = [jnp.zeros((8, T), F32) for _ in range(4)]
     for n in range(NT):
@@ -552,18 +617,26 @@
         mean_n = tile[:8, :]
         spread_n = tile[8:, :] + onoise[n : n + 1, :]
         for j in range(4):
-            hit = otile[:, j : j + 1] == n
+            hit = tiles[j] == float(n)
             picked_mean[j] = jnp.where(hit, mean_n, picked_mean[j])
             picked_spread[j] = jnp.where(hit, spread_n, picked_spread[j])
     for j in range(4):
         value = (oval[:, j, :] - picked_mean[j]) / picked_spread[j]
-        o_in[:, j, :] = jnp.where(ocount[...] > j, value, 0.0)
+        o_in[:, j, :] = jnp.where(counts > j + 0.5, value, 0.0)
 
     def vbody(o, _):
         gather_copy(o).wait_send()
         return 0
 
     lax.fori_loop(1, 16, vbody, 0)
+
+
+def emit(cov, mean, sm, ss, inn, o_cov, o_mean, o_sm, o_ss, o_in):
+    o_cov[...] = cov[...]
+    o_mean[...] = mean[...].astype(BF16)
+    o_sm[...] = sm[...]
+    o_ss[...] = ss[...]
+    o_in[...] = inn[...]
 
 
 def shards(
@@ -571,7 +644,7 @@
     step_offset, step_var, obs_tiles, obs_count, obs_value, obs_noise,
 ):
     vmem = pl.BlockSpec(memory_space=pltpu.VMEM)
-    hbm = pl.BlockSpec(memory_space=pl.ANY)
+    hbm = pl.BlockSpec(memory_space=pltpu.HBM)
     dma = pltpu.SemaphoreType.DMA
     out_cov, out_mean, step_mean, step_spread, innovation = pl.pallas_call(
         kernel,
@@ -582,7 +655,7 @@
             jax.ShapeDtypeStruct((8, RB), F32),
             jax.ShapeDtypeStruct((8, 4, T), F32),
         ),
-        in_specs=[vmem, vmem, vmem, vmem, hbm, hbm, vmem, vmem, vmem, vmem, vmem, vmem],
+        in_specs=[hbm] * 12,
         out_specs=(vmem,) * 5,
         scratch_shapes=[
             pltpu.VMEM((N, N), BF16),
@@ -600,26 +673,49 @@
             pltpu.VMEM((NT, KEEP * T, T), BF16),
             pltpu.VMEM((T, N), F32),
             pltpu.VMEM((512, T), F32),
+            pltpu.VMEM((1, 512), F32),
             pltpu.VMEM((RB, N), BF16),
             pltpu.VMEM((16, N), BF16),
             pltpu.VMEM((16, N), BF16),
             pltpu.VMEM((16, 16, T), F32),
             pltpu.VMEM((RB, N), BF16),
             pltpu.VMEM((RB, N), BF16),
-            dma((5, 16)), dma((5, 17)), dma((5, 16)), dma((5, 16)),
+            pltpu.VMEM((1, RB, N), BF16),
+            pltpu.VMEM((1, RB), F32),
+            pltpu.VMEM((1, RB, N), BF16),
+            pltpu.VMEM((8, RB), BF16),
+            pltpu.VMEM((8, RB), F32),
+            pltpu.VMEM((8, RB), F32),
+            pltpu.VMEM((4, 8), jnp.int32),
+            pltpu.VMEM((1, 8), jnp.int32),
+            pltpu.VMEM((8, 4, T), F32),
+            pltpu.VMEM((NT, T), F32),
+            dma((10,)),
+            dma((NPARTS, 16)), dma((NPARTS, 17)), dma((5, 16)), dma((5, 16)),
             dma((2,)), dma((3,)), dma((8,)), dma((KEEP,)),
             dma((8,)), dma((8,)), dma((8,)), dma((8,)),
             dma((1,)), dma((1,)), dma((1,)), dma((1,)),
             dma((16,)), dma((16,)),
         ],
         compiler_params=pltpu.CompilerParams(
-            collective_id=0, has_side_effects=True, vmem_limit_bytes=48 * 2**20
+            collective_id=0, has_side_effects=True, vmem_limit_bytes=66 * 10**6
         ),
     )(
         seg_gain, seg_offset, seg_noise, end_mean, end_cov, step_gain,
-        step_offset, step_var, obs_tiles, obs_count.reshape(8, 1), obs_value, obs_noise.reshape(NT, T),
+        step_offset, step_var, obs_tiles.T, obs_count.reshape(1, 8), obs_value, obs_noise.reshape(NT, T),
     )
-    return out_cov, out_mean.astype(BF16), step_mean, step_spread, innovation
+    return pl.pallas_call(
+        emit,
+        out_shape=(
+            jax.ShapeDtypeStruct((1, RB, N), BF16),
+            jax.ShapeDtypeStruct((1, RB), BF16),
+            jax.ShapeDtypeStruct((8, RB), F32),
+            jax.ShapeDtypeStruct((8, RB), F32),
+            jax.ShapeDtypeStruct((8, 4, T), F32),
+        ),
+        in_specs=[vmem] * 5,
+        out_specs=(vmem,) * 5,
+    )(out_cov, out_mean, step_mean, step_spread, innovation)
 
 
 def solution(mesh):

time: 102 us -> 90.7 us (0.89)
  local copies, waits for them, and re-layouts: 9.59 us -> 0 us
    unnamed x25 -> x0, local copies, waits for them, and re-layouts: 8.86 us -> none
    pallas_call x1, Pallas kernels: 90.8 us -> 88.3 us  [shards(): pl.pallas_call(kernel, out_shape=(jax.ShapeDtypeStruct((1, RB, N), BF16),...]
    pallas_call x0 -> x1, Pallas kernels: none -> 1.59 us  [shards(): pl.pallas_call(emit, out_shape=(jax.ShapeDtypeStruct((1, RB, N), BF16), j...]
where the time goes in v2:
time: 90.7 us; the launch traced here: 90.5 us
  Pallas kernels  89.9 us (99%)
    pallas_call x1, Pallas kernels, shards(): pl.pallas_call(kernel, out_shape=(jax.ShapeDtypeStruct((1, RB, N), BF16),...  88.3 us

profile of v2, /device:TPU:1, one launch (start us, length us, event | category | flops | bytes accessed | tf_op | source)
XLA Modules:
  0.0 90.5 jit_solution(2162983387326350138)
XLA Ops:
  0.6 88.3 %shard_map.155 = (bf16[1,64,1024]{2,1,0:T(8,128)(2,1)}, f32[1,64]{1,0:T(1,128)}, f32[8,64]{1,0:T(8,128)}, f32[8,64]{1,0:T(8,128)}, f32[8,4,128]{2,1,0:T(4,128)}) custom-call(bf16[1,64,1024]{2,1,0:T(8,128)(2,1)} %gain_h.1, f32[1,64]{1,0:T(1,128)} %off_h.1, bf16[1,64,1024]{2,1,0:T(8,128)(2,1)} %noise_h.1, bf16[8,64]{1,0:T(8,128)(2,1)} %emean_h.1, ...), custom_call_target="tpu_custom_call" | custom-call | tf_op jit(solution)/shard_map/pallas_call | solution.py:649
  88.9 1.6 %shard_map.156 = (bf16[1,64,1024]{2,1,0:T(8,128)(2,1)}, bf16[1,64]{1,0:T(2,128)(2,1)}, f32[8,64]{1,0:T(8,128)}, f32[8,64]{1,0:T(8,128)}, f32[8,4,128]{2,1,0:T(4,128)}) custom-call(bf16[1,64,1024]{2,1,0:T(8,128)(2,1)} %get-tuple-element.10.cov, f32[1,64]{1,0:T(1,128)} %get-tuple-element.11.mean, f32[8,64]{1,0:T(8,128)} %get-tuple-element.12.sm, ...), custom_call_target="tpu_custom_call" | custom-call | tf_op jit(solution)/shard_map/pallas_call | solution.py:707

commit v3 on v2

--- a/solution.py
+++ b/solution.py
@@ -21,8 +21,8 @@
 PARTS = {i: tuple(range(i * CG, (i + 1) * CG)) for i in (GA, GB, GC)}
 PARTS |= {i: tuple(range(3 * CG + (i - S0) * CS, 3 * CG + (i - S0 + 1) * CS)) for i in (S0, S1)}
 S_CUTS = {1: ((0, SROWS),), 2: ((0, 176), (176, 160))}[CS]
-LAG_B = 1
-LAG_C = 2
+LAG_B = 2
+LAG_C = 4
 
 
 def nn(x, y):

time: 90.7 us -> 86.7 us (0.956)
  Pallas kernels: 89.9 us -> 85.2 us
    pallas_call x1, Pallas kernels: 88.3 us -> 83.6 us  [shards(): pl.pallas_call(kernel, out_shape=(jax.ShapeDtypeStruct((1, RB, N), BF16),...]
where the time goes in v3:
time: 86.7 us; the launch traced here: 85.9 us
  Pallas kernels  85.2 us (98%)
    pallas_call x1, Pallas kernels, shards(): pl.pallas_call(kernel, out_shape=(jax.ShapeDtypeStruct((1, RB, N), BF16),...  83.6 us

profile of v3, /device:TPU:1, one launch (start us, length us, event | category | flops | bytes accessed | tf_op | source)
XLA Modules:
  0.0 85.9 jit_solution(7104541213569231)
XLA Ops:
  0.6 83.6 %shard_map.155 = (bf16[1,64,1024]{2,1,0:T(8,128)(2,1)}, f32[1,64]{1,0:T(1,128)}, f32[8,64]{1,0:T(8,128)}, f32[8,64]{1,0:T(8,128)}, f32[8,4,128]{2,1,0:T(4,128)}) custom-call(bf16[1,64,1024]{2,1,0:T(8,128)(2,1)} %gain_h.1, f32[1,64]{1,0:T(1,128)} %off_h.1, bf16[1,64,1024]{2,1,0:T(8,128)(2,1)} %noise_h.1, bf16[8,64]{1,0:T(8,128)(2,1)} %emean_h.1, ...), custom_call_target="tpu_custom_call" | custom-call | tf_op jit(solution)/shard_map/pallas_call | solution.py:649
  84.3 1.6 %shard_map.156 = (bf16[1,64,1024]{2,1,0:T(8,128)(2,1)}, bf16[1,64]{1,0:T(2,128)(2,1)}, f32[8,64]{1,0:T(8,128)}, f32[8,64]{1,0:T(8,128)}, f32[8,4,128]{2,1,0:T(4,128)}) custom-call(bf16[1,64,1024]{2,1,0:T(8,128)(2,1)} %get-tuple-element.10.cov, f32[1,64]{1,0:T(1,128)} %get-tuple-element.11.mean, f32[8,64]{1,0:T(8,128)} %get-tuple-element.12.sm, ...), custom_call_target="tpu_custom_call" | custom-call | tf_op jit(solution)/shard_map/pallas_call | solution.py:707
